TPU v7x, 512 devices: a whole 4x4x16 slice. The times are simulated.
512 devices in a mesh: dp: 16 (over x, z_hi, core), tm: 8 (over z_lo), height: 4 (over y).
Axes of the slice: x: 4, y: 4, z: 16 (z_hi: 2, z_lo: 8; z = z_hi * 8 + z_lo), core: 2. Of those that a mesh axis runs over, the one named last changes fastest.
Arguments:
- latent: bfloat16 [256, 8, 16, 512], P(('dp', 'tm'), None, None, 'height'), parts along dimension 0, may hold values from -6 to 6
- gain_latent: float32 [512], P('height'), may hold values from 0.25 to 1.75
- shift_latent: float32 [512], P('height'), may hold values from -3 to 3
- conv_latent: bfloat16 [13824, 512], P('tm', 'height'), may hold values from -0.0546875 to 0.0546875
- up_weight: bfloat16 [512, 2048], P('height'), may hold values from -0.25 to 0.25
- gain_block: float32 [256], replicated, may hold values from 0.25 to 1.75
- shift_block: float32 [256], replicated, may hold values from -3 to 3
- conv_block: bfloat16 [6912, 256], P(('tm', 'height')), may hold values from -0.078125 to 0.078125
- cotangent: bfloat16 [512, 16, 32, 256], P(('dp', 'tm'), 'height'), parts along dimension 0, may hold values from -6 to 6
Outputs:
- decoded: bfloat16 [512, 16, 32, 256], P(('dp', 'tm'), 'height'), parts along dimension 0
- grad_upsampled: bfloat16 [512, 16, 32, 256], P(('dp', 'tm'), 'height'), parts along dimension 0
- grad_weight: float32 [36864, 256], P(('dp', 'tm', 'height')), parts along dimension 0
- grad_gain: float32 [4096], P('dp'), parts along dimension 0
- grad_shift: float32 [4096], P('dp'), parts along dimension 0
There are 16 independent parts, one for each index of `dp`. A program takes and returns all parts, laid end to end along the dimension named above; an argument that names none is the same for every part. Nothing has to cross between parts.
All inputs are finite; a program needn't handle non-finite values.
Results may differ from a plain program's by a relative error of at most 0.009.
Values may be sent and summed in bfloat16 or wider, within the bound.
No kernel may reach another device: no remote copies, remote signals or barrier semaphores. Data moves between devices by JAX's collectives and lax.ppermute only.
A program may use at most 128 MiB of HBM per device.

v0:
```python
import jax
import jax.numpy as jnp
from jax import lax
from jax.sharding import PartitionSpec as P

C1 = 512
GROUPS = 32
epsilon = 1e-06


def copy_for_each(array, axis):
    devices = lax.axis_size(axis)
    return lax.all_to_all(
        jnp.broadcast_to(array[None], (devices, *array.shape)), axis, 0, 0, tiled=True
    )


def taken_together(array, axis):
    everything = copy_for_each(array, axis)
    return jnp.sum(everything, axis=0)


def packed_total(arrays, axis):
    ends = [0]
    for a in arrays:
        ends.append(ends[-1] + a.size)
    so_far = taken_together(jnp.concatenate([a.ravel() for a in arrays]), axis)
    return tuple((so_far[b:e].reshape(a.shape) for a, b, e in zip(arrays, ends, ends[1:])))


def shifted(block, axis, distance):
    devices = range(lax.axis_size(axis))
    route = [(i - distance, i) for i in devices if i - distance in devices]
    return lax.ppermute(block, axis, route)


def in_order(tiles, dim):
    tiles = jnp.moveaxis(tiles, 0, dim)
    shape = tiles.shape
    return tiles.reshape(*shape[:dim], shape[dim] * shape[dim + 1], *shape[dim + 2 :])


def gather_directly(array, axis, dim):
    tiles = copy_for_each(array, axis)
    return in_order(tiles, dim)


def extended_2(cells, sides, width):
    for axis, dim in sides:
        count = lax.axis_size(axis)
        ends = count - 1
        head = lax.slice_in_dim(cells, 0, width, axis=dim)
        tail = lax.slice_in_dim(cells, cells.shape[dim] - width, cells.shape[dim], axis=dim)
        cells = jnp.concatenate(
            [
                lax.ppermute(tail, axis, [(i, (i + 1) % count) for i in range(ends)]),
                cells,
                lax.ppermute(head, axis, [((i + 1) % count, i) for i in range(ends)]),
            ],
            axis=dim,
        )
    return cells


def gather_in_order(array, axes, turns):
    tiles = array
    for k in turns:
        tiles = lax.all_gather(tiles, axes[k])
    done = turns[::-1]
    back = [done.index(k) for k in range(len(axes))]
    tiles = tiles.transpose(*back, *range(len(axes), tiles.ndim))
    return tiles.reshape(-1, *array.shape)


def whole_of(array, axes, turns, dim):
    return in_order(gather_in_order(array, axes, turns), dim)


def cut_along(array, dim, devices):
    before, after = (array.shape[:dim], array.shape[dim + 1 :])
    return jnp.moveaxis(array.reshape(*before, devices, -1, *after), dim, 0)


def sum_at_owner(array, axis, dim):
    tiles = cut_along(array, dim, lax.axis_size(axis))
    arrived = lax.all_to_all(tiles, axis, split_axis=0, concat_axis=0, tiled=True)
    return arrived.sum(axis=0)


def standardize(values, mean_value, inverse, groups):
    shape_full = values.shape
    grouped = values.reshape(shape_full[:-1] + (groups, shape_full[-1] // groups))
    return ((grouped - mean_value[:, None]) * inverse[:, None]).reshape(shape_full)


def causal_taps(padded, weight, frames, rows, cols):
    channels_in = padded.shape[-1]
    summed = jnp.zeros((frames * rows * cols, weight.shape[1]), jnp.float32)
    for lag_step in range(3):
        for row_step in range(3):
            for col_step in range(3):
                tap_index = (lag_step * 3 + row_step) * 3 + col_step
                window = padded[
                    lag_step : lag_step + frames,
                    row_step : row_step + rows,
                    col_step : col_step + cols,
                ]
                kernel = weight[tap_index * channels_in : (tap_index + 1) * channels_in]
                summed = summed + jnp.dot(
                    window.reshape(-1, channels_in), kernel, preferred_element_type=jnp.float32
                )
    return summed.reshape(frames, rows, cols, weight.shape[1])


def transposed_taps(padded, weight, frames, rows, cols):
    channels_out = padded.shape[-1]
    channels_in = weight.shape[0] // 27
    summed = jnp.zeros((frames * rows * cols, channels_in), jnp.float32)
    for lag_step in range(3):
        for row_step in range(3):
            for col_step in range(3):
                tap_index = (lag_step * 3 + row_step) * 3 + col_step
                window = padded[
                    2 - lag_step : 2 - lag_step + frames,
                    2 - row_step : 2 - row_step + rows,
                    2 - col_step : 2 - col_step + cols,
                ]
                kernel = weight[tap_index * channels_in : (tap_index + 1) * channels_in]
                summed = summed + lax.dot_general(
                    window.reshape(-1, channels_out),
                    kernel,
                    (((1,), (1,)), ((), ())),
                    preferred_element_type=jnp.float32,
                )
    return summed.reshape(frames, rows, cols, channels_in)


def weight_terms(padded, grads, frames, rows, cols):
    channels_in = padded.shape[-1]
    flat_grads = grads.reshape(-1, grads.shape[-1])
    blocks = []
    for row_step in range(3):
        for col_step in range(3):
            window = padded[2 : 2 + frames, row_step : row_step + rows, col_step : col_step + cols]
            blocks.append(
                lax.dot_general(
                    window.reshape(-1, channels_in),
                    flat_grads,
                    (((0,), (0,)), ((), ())),
                    preferred_element_type=jnp.float32,
                )
            )
    return jnp.concatenate(blocks, 0)


def local(
    latent,
    gain_latent,
    shift_latent,
    conv_latent,
    up_weight,
    gain_block,
    shift_block,
    conv_block,
    cotangent,
):
    per_group = C1 // GROUPS
    groups_here = latent.shape[-1] // per_group
    latent_f32 = latent.astype(jnp.float32)
    grouped = latent_f32.reshape(-1, groups_here, per_group)
    first_sums = jnp.sum(grouped, axis=(0, 2))
    second_sums = jnp.sum(grouped * grouped, axis=(0, 2))
    first_totals, second_totals = packed_total((first_sums, second_sums), "tm")
    count_latent = grouped.shape[0] * per_group * lax.axis_size("tm")
    mean_latent = first_totals / count_latent
    inverse_latent = lax.rsqrt(second_totals / count_latent - mean_latent * mean_latent + epsilon)
    normed = (
        standardize(latent_f32, mean_latent, inverse_latent, groups_here) * gain_latent
        + shift_latent
    )
    active = jax.nn.silu(normed).astype(jnp.bfloat16)
    earlier = shifted(active, "tm", 1)
    extended = jnp.concatenate([earlier, active], 0)
    all_channels = gather_directly(extended, "height", 3)
    padded = jnp.pad(all_channels, ((0, 0), (1, 1), (1, 1), (0, 0)))
    latent_weight = lax.all_gather(conv_latent, "tm", axis=0, tiled=True)
    frames_latent, rows_latent, cols_latent = (latent.shape[0], latent.shape[1], latent.shape[2])
    mixed = causal_taps(padded, latent_weight, frames_latent, rows_latent, cols_latent)
    refined = (latent_f32 + mixed).astype(jnp.bfloat16)
    band_rows = rows_latent // lax.axis_size("height")
    own_band = lax.all_to_all(refined, "height", split_axis=1, concat_axis=3, tiled=True)
    flat_band = own_band.reshape(-1, own_band.shape[-1])
    expanded = jnp.dot(
        flat_band, gather_directly(up_weight, "height", 0), preferred_element_type=jnp.float32
    )
    channels_block = up_weight.shape[1] // 8
    spread = expanded.reshape(frames_latent, band_rows, cols_latent, 2, 2, 2, channels_block)
    spread = spread.transpose(0, 3, 1, 4, 2, 5, 6)
    upsampled = spread.reshape(
        2 * frames_latent, 2 * band_rows, 2 * cols_latent, channels_block
    ).astype(jnp.bfloat16)
    frames_block, rows_block, cols_block = (
        upsampled.shape[0],
        upsampled.shape[1],
        upsampled.shape[2],
    )
    up_f32 = upsampled.astype(jnp.float32)
    per_block = channels_block // GROUPS
    grouped_block = up_f32.reshape(-1, GROUPS, per_block)
    block_first = jnp.sum(grouped_block, axis=(0, 2))
    block_second = jnp.sum(grouped_block * grouped_block, axis=(0, 2))
    block_first, block_second = packed_total((block_first, block_second), ("tm", "height"))
    count_block = grouped_block.shape[0] * per_block * lax.axis_size("tm") * lax.axis_size("height")
    mean_block = block_first / count_block
    inverse_block = lax.rsqrt(block_second / count_block - mean_block * mean_block + epsilon)
    standard = standardize(up_f32, mean_block, inverse_block, GROUPS)
    normed_block = standard * gain_block + shift_block
    active_block = jax.nn.silu(normed_block).astype(jnp.bfloat16)
    before = shifted(active_block[-2:], "tm", 1)
    ext_block = jnp.concatenate([before, active_block], 0)
    beside_all = extended_2(ext_block, (("height", 1),), 1)
    padded_block = jnp.pad(beside_all, ((0, 0), (0, 0), (1, 1), (0, 0)))
    block_weight = whole_of(conv_block, ("tm", "height"), (0, 1), 0)
    mixed_block = causal_taps(padded_block, block_weight, frames_block, rows_block, cols_block)
    decoded = (up_f32 + mixed_block).astype(jnp.bfloat16)
    after = shifted(cotangent[:2], "tm", -1)
    grad_ext = jnp.concatenate([cotangent, after], 0)
    grad_around = extended_2(grad_ext, (("height", 1),), 1)
    grad_padded = jnp.pad(grad_around, ((0, 0), (0, 0), (1, 1), (0, 0)))
    grad_active = transposed_taps(grad_padded, block_weight, frames_block, rows_block, cols_block)
    local_terms = weight_terms(padded_block, cotangent, frames_block, rows_block, cols_block)
    time_summed = sum_at_owner(local_terms, "tm", 0)
    grad_weight = sum_at_owner(time_summed, "height", 0)
    sigmoid = jax.nn.sigmoid(normed_block)
    grad_normed = grad_active * sigmoid * (1.0 + normed_block * (1.0 - sigmoid))
    flat_grad = grad_normed.reshape(-1, channels_block)
    flat_standard = standard.reshape(-1, channels_block)
    grad_shift, grad_gain = packed_total(
        (jnp.sum(flat_grad, axis=0), jnp.sum(flat_grad * flat_standard, axis=0)), ("tm", "height")
    )
    first_mean = jnp.sum((gain_block * grad_shift).reshape(GROUPS, per_block), axis=1) / count_block
    second_mean = jnp.sum((gain_block * grad_gain).reshape(GROUPS, per_block), axis=1) / count_block
    grouped_grad = (grad_normed * gain_block).reshape(-1, GROUPS, per_block)
    grouped_standard = standard.reshape(-1, GROUPS, per_block)
    corrected = (
        grouped_grad - first_mean[:, None] - grouped_standard * second_mean[:, None]
    ) * inverse_block[:, None]
    grad_upsampled = (cotangent.astype(jnp.float32) + corrected.reshape(cotangent.shape)).astype(
        jnp.bfloat16
    )
    return (decoded, grad_upsampled, grad_weight, grad_gain, grad_shift)


def solution(mesh):
    return jax.shard_map(
        local,
        mesh=mesh,
        in_specs=(
            P(("dp", "tm"), None, None, "height"),
            P("height"),
            P("height"),
            P("tm", "height"),
            P("height", None),
            P(),
            P(),
            P(("tm", "height"), None),
            P(("dp", "tm"), "height", None, None),
        ),
        out_specs=(
            P(("dp", "tm"), "height", None, None),
            P(("dp", "tm"), "height", None, None),
            P(("dp", "tm", "height"), None),
            P("dp"),
            P("dp"),
        ),
        check_vma=False,
    )
```

profile of v0, /device:TPU:2, one launch (start us, length us, event | category | flops | bytes accessed | tf_op | source)
XLA Modules:
  0.0 456.5 jit_solution(3244054950084139941)
XLA Ops:
  7.2 54.2 %all-gather = bf16[1728,256]{1,0:T(8,128)(2,1)} all-gather(bf16[216,256]{1,0:T(8,128)(2,1)} %param.16), channel_id=2, replica_groups=mesh['dp'=16,'tm'=8,'height'=4] {'tm'}, dimensions={0}, use_global_device_ids=true | all-gather | bytes 995328 | tf_op jit(solution)/shard_map/all_gather | solution.py:68
  63.4 10.3 %all-to-all-start = ((f32[8,1,16]{2,1,0:T(1,128)}), f32[8,1,16]{2,1,0:T(1,128)S(1)}, u32[]{:S(2)}, u32[]{:S(2)}) async-start(f32[8,1,16]{2,1,0:T(1,128)} %broadcast_in_dim.10), calls=%async_computation | async-start | bytes 8192 | tf_op jit(solution)/shard_map/all_to_all | solution.py:13
  75.9 8.1 %all-to-all-done = f32[8,1,16]{2,1,0:T(1,128)S(1)} async-done(((f32[8,1,16]{2,1,0:T(1,128)}), f32[8,1,16]{2,1,0:T(1,128)S(1)}, u32[]{:S(2)}, u32[]{:S(2)}) %all-to-all-start) | async-done | bytes 544 | tf_op jit(solution)/shard_map/all_to_all | solution.py:13
  90.7 4.5 all-to-all-start.1
  96.5 4.6 collective-permute-start.5
  101.4 8.3 %all-to-all-done.1 = bf16[4,4,8,16,128]{4,3,2,1,0:T(8,128)(2,1)S(1)} async-done(((bf16[4,4,8,16,128]{4,3,2,1,0:T(8,128)(2,1)}), bf16[4,4,8,16,128]{4,3,2,1,0:T(8,128)(2,1)S(1)}, u32[]{:S(2)}, u32[]{:S(2)}) %all-to-all-start.1) | async-done | bytes 524320 | tf_op jit(solution)/shard_map/all_to_all | solution.py:13
  111.3 3.6 all-to-all-start.3
  125.4 19.1 %all-to-all-done.3 = bf16[4,128,2048]{1,2,0:T(8,128)(2,1)S(1)} async-done(((bf16[4,128,2048]{1,2,0:T(8,128)(2,1)}), bf16[4,128,2048]{1,2,0:T(8,128)(2,1)S(1)}, u32[]{:S(2)}, u32[]{:S(2)}) %all-to-all-start.3) | async-done | bytes 2097184 | tf_op jit(solution)/shard_map/all_to_all | solution.py:13
  144.5 2.6 copy.75
  147.2 3.9 copy.76
  161.2 68.7 %all-gather.5.cloned.1.call-done = bf16[13824,128]{1,0:T(8,128)(2,1)} async-done(((bf16[1728,128]{1,0:T(8,128)(2,1)}), bf16[13824,128]{1,0:T(8,128)(2,1)}) %all-gather.5.cloned.1.call-update) | async-done | bytes 3538960 | tf_op jit(solution)/shard_map/all_gather | solution.py:186
  245.2 4.2 all-to-all-start.2
  251.6 3.6 all-to-all-done.2
  258.2 3.7 fusion.146
  266.1 4.8 %all-to-all-start.4 = ((f32[32,1,64]{2,1,0:T(1,128)}), f32[32,1,64]{2,1,0:T(1,128)S(1)}, u32[]{:S(2)}, u32[]{:S(2)}) async-start(f32[32,1,64]{2,1,0:T(1,128)} %broadcast_in_dim.13), calls=%async_computation.4 | async-start | bytes 32768 | tf_op jit(solution)/shard_map/all_to_all | solution.py:13
  277.4 5.9 %all-to-all-done.4 = f32[32,1,64]{2,1,0:T(1,128)S(1)} async-done(((f32[32,1,64]{2,1,0:T(1,128)}), f32[32,1,64]{2,1,0:T(1,128)S(1)}, u32[]{:S(2)}, u32[]{:S(2)}) %all-to-all-start.4) | async-done | bytes 8224 | tf_op jit(solution)/shard_map/all_to_all | solution.py:13
  287.1 2.8 fusion.145
  290.6 6.5 %all-to-all-start.5 = ((f32[32,1,512]{2,1,0:T(1,128)}), f32[32,1,512]{2,1,0:T(1,128)S(1)}, u32[]{:S(2)}, u32[]{:S(2)}) async-start(f32[32,1,512]{2,1,0:T(1,128)} %broadcast_in_dim.14), calls=%async_computation.5 | async-start | bytes 131072 | tf_op jit(solution)/shard_map/all_to_all | solution.py:13
  298.5 11.5 %all-to-all-done.5 = f32[32,1,512]{2,1,0:T(1,128)S(1)} async-done(((f32[32,1,512]{2,1,0:T(1,128)}), f32[32,1,512]{2,1,0:T(1,128)S(1)}, u32[]{:S(2)}, u32[]{:S(2)}) %all-to-all-start.5) | async-done | bytes 65568 | tf_op jit(solution)/shard_map/all_to_all | solution.py:13
  319.8 4.6 collective-permute-start.2
  330.8 5.2 %all-to-all-start.6 = ((f32[8,288,256]{2,1,0:T(8,128)}), f32[8,288,256]{2,1,0:T(8,128)S(1)}, u32[]{:S(2)}, u32[]{:S(2)}) async-start(f32[8,288,256]{2,1,0:T(8,128)} %bitcast.329), calls=%async_computation.6 | async-start | bytes 4718592 | tf_op jit(solution)/shard_map/all_to_all | solution.py:86
  345.7 91.6 %all-to-all-done.6 = f32[8,288,256]{2,1,0:T(8,128)S(1)} async-done(((f32[8,288,256]{2,1,0:T(8,128)}), f32[8,288,256]{2,1,0:T(8,128)S(1)}, u32[]{:S(2)}, u32[]{:S(2)}) %all-to-all-start.6) | async-done | bytes 2359328 | tf_op jit(solution)/shard_map/all_to_all | solution.py:86
  438.2 4.0 all-to-all-start.7
  443.0 6.1 %all-to-all-done.7 = f32[4,72,256]{2,1,0:T(8,128)S(1)} async-done(((f32[4,72,256]{2,1,0:T(8,128)}), f32[4,72,256]{2,1,0:T(8,128)S(1)}, u32[]{:S(2)}, u32[]{:S(2)}) %all-to-all-start.7) | async-done | bytes 294944 | tf_op jit(solution)/shard_map/all_to_all | solution.py:86
  (305 shorter events, 98.6 us)
Async XLA Ops:
  7.2 93.9 %copy-start.53 = (bf16[128,2048]{1,0:T(8,128)(2,1)S(1)}, bf16[128,2048]{1,0:T(8,128)(2,1)}, u32[]{:S(2)}) copy-start(bf16[128,2048]{1,0:T(8,128)(2,1)} %param.13) | copy-start | bytes 1572868
  7.2 143.9 %all-gather.7.cloned.1.call-start = ((), (), s32[]{:S(2)}) async-start(), calls=%async_computation.9 | async-start | bytes 4423680 | tf_op jit(solution)/shard_map/all_gather | solution.py:68
  63.4 20.6 %all-to-all-start = ((f32[8,1,16]{2,1,0:T(1,128)}), f32[8,1,16]{2,1,0:T(1,128)S(1)}, u32[]{:S(2)}, u32[]{:S(2)}) async-start(f32[8,1,16]{2,1,0:T(1,128)} %broadcast_in_dim.10), calls=%async_computation | async-start | bytes 8192 | tf_op jit(solution)/shard_map/all_to_all | solution.py:13
  74.6 20.5 %collective-permute-start.4 = (bf16[2,4,32,256]{3,2,1,0:T(8,128)(2,1)S(1)}, bf16[2,4,32,256]{3,2,1,0:T(8,128)(2,1)S(1)}, u32[]{:S(2)}, u32[]{:S(2)}) collective-permute-start(bf16[2,4,32,256]{3,2,1,0:T(8,128)(2,1)S(1)} %slice.629), channel_id=1, source_target_pairs={{4,0},{8,4},{12,8},{16,12},{20,16},{24,20},{28,24},{5,1},{9,5},{13... | collective-permute-start | bytes 393224 | tf_op jit(solution)/shard_map/ppermute | solution.py:34
  85.3 4.4 collective-permute-start
  90.7 18.9 %all-to-all-start.1 = ((bf16[4,4,8,16,128]{4,3,2,1,0:T(8,128)(2,1)}), bf16[4,4,8,16,128]{4,3,2,1,0:T(8,128)(2,1)S(1)}, u32[]{:S(2)}, u32[]{:S(2)}) async-start(bf16[4,4,8,16,128]{4,3,2,1,0:T(8,128)(2,1)} %broadcast_in_dim.11), calls=%async_computation.1 | async-start | bytes 1048576 | tf_op jit(solution)/shard_map/all_to_all | solution.py:13
  95.1 134.7 %all-gather.5.cloned.1.call-start = ((), (), s32[]{:S(2)}) async-start(), calls=%async_computation.8 | async-start | bytes 3981312 | tf_op jit(solution)/shard_map/all_gather | solution.py:186
  95.2 19.7 %collective-permute-start.6 = (bf16[6,1,32,256]{3,2,1,0:T(8,128)(2,1)S(1)}, bf16[6,1,32,256]{3,2,1,0:T(8,128)(2,1)S(1)}, u32[]{:S(2)}, u32[]{:S(2)}) collective-permute-start(bf16[6,1,32,256]{3,2,1,0:T(8,128)(2,1)S(1)} %get-tuple-element.98), channel_id=1, source_target_pairs={{1,0},{2,1},{3,2},{5,4},{6,5},{7,6},{9,8},{10,9},{11,10},{13,12},{... | collective-permute-start | bytes 294920 | tf_op jit(solution)/shard_map/ppermute | solution.py:58
  96.5 18.4 %collective-permute-start.5 = (bf16[6,1,32,256]{3,2,1,0:T(8,128)(2,1)S(1)}, bf16[6,1,32,256]{3,2,1,0:T(8,128)(2,1)S(1)}, u32[]{:S(2)}, u32[]{:S(2)}) collective-permute-start(bf16[6,1,32,256]{3,2,1,0:T(8,128)(2,1)S(1)} %get-tuple-element.97), channel_id=1, source_target_pairs={{0,1},{1,2},{2,3},{4,5},{5,6},{6,7},{8,9},{9,10},{10,11},{12,13},{... | collective-permute-start | bytes 294920 | tf_op jit(solution)/shard_map/ppermute | solution.py:56
  111.3 33.2 %all-to-all-start.3 = ((bf16[4,128,2048]{1,2,0:T(8,128)(2,1)}), bf16[4,128,2048]{1,2,0:T(8,128)(2,1)S(1)}, u32[]{:S(2)}, u32[]{:S(2)}) async-start(bf16[4,128,2048]{1,2,0:T(8,128)(2,1)} %broadcast_in_dim.12), calls=%async_computation.3 | async-start | bytes 4194304 | tf_op jit(solution)/shard_map/all_to_all | solution.py:13
  153.5 133.6 %copy-start = (bf16[8,4,216,256]{3,2,1,0:T(8,128)(2,1)}, bf16[8,4,216,256]{3,2,1,0:T(8,128)(2,1)S(1)}, u32[]{:S(2)}) copy-start(bf16[8,4,216,256]{3,2,1,0:T(8,128)(2,1)S(1)} %copy.79) | copy-start | bytes 10616836
  245.2 10.0 %all-to-all-start.2 = ((bf16[2,8,16,128]{3,2,0,1:T(8,128)(2,1)}), bf16[2,8,16,128]{3,2,0,1:T(8,128)(2,1)}, u32[]{:S(2)}, u32[]{:S(2)}) async-start(bf16[2,8,16,128]{3,2,0,1:T(8,128)(2,1)} %fusion.45), calls=%async_computation.2 | async-start | bytes 131072 | tf_op jit(solution)/shard_map/all_to_all | solution.py:191
  266.1 17.1 %all-to-all-start.4 = ((f32[32,1,64]{2,1,0:T(1,128)}), f32[32,1,64]{2,1,0:T(1,128)S(1)}, u32[]{:S(2)}, u32[]{:S(2)}) async-start(f32[32,1,64]{2,1,0:T(1,128)} %broadcast_in_dim.13), calls=%async_computation.4 | async-start | bytes 32768 | tf_op jit(solution)/shard_map/all_to_all | solution.py:13
  287.1 24.3 %copy-start.59 = (f32[256]{0:T(256)S(1)}, f32[256]{0:T(256)}, u32[]{:S(2)}) copy-start(f32[256]{0:T(256)} %sub.74) | copy-start | bytes 3076
  287.1 24.3 %copy-start.60 = (f32[256]{0:T(256)S(1)}, f32[256]{0:T(256)}, u32[]{:S(2)}) copy-start(f32[256]{0:T(256)} %param.15) | copy-start | bytes 3076
  289.9 37.0 %copy-start.8 = (bf16[4,4,32,256]{3,2,1,0:T(8,128)(2,1)S(1)}, bf16[4,4,32,256]{3,2,1,0:T(8,128)(2,1)}, u32[]{:S(2)}) copy-start(bf16[4,4,32,256]{3,2,1,0:T(8,128)(2,1)} %param.17) | copy-start | bytes 786436
  290.6 19.4 %all-to-all-start.5 = ((f32[32,1,512]{2,1,0:T(1,128)}), f32[32,1,512]{2,1,0:T(1,128)S(1)}, u32[]{:S(2)}, u32[]{:S(2)}) async-start(f32[32,1,512]{2,1,0:T(1,128)} %broadcast_in_dim.14), calls=%async_computation.5 | async-start | bytes 131072 | tf_op jit(solution)/shard_map/all_to_all | solution.py:13
  298.5 26.5 %copy-start.4 = (f32[4,4,32,256]{3,2,1,0:T(8,128)}, f32[4,4,32,256]{3,2,1,0:T(8,128)S(1)}, u32[]{:S(2)}) copy-start(f32[4,4,32,256]{3,2,1,0:T(8,128)S(1)} %reshape.484) | copy-start | bytes 1572868
  313.6 4.8 %collective-permute-start.1 = (bf16[2,4,32,256]{3,2,1,0:T(8,128)(2,1)S(1)}, bf16[2,4,32,256]{3,2,1,0:T(8,128)(2,1)S(1)}, u32[]{:S(2)}, u32[]{:S(2)}) collective-permute-start(bf16[2,4,32,256]{3,2,1,0:T(8,128)(2,1)S(1)} %slice.690), channel_id=1, source_target_pairs={{0,4},{4,8},{8,12},{12,16},{16,20},{20,24},{24,28},{1,5},{5,9},{9,... | collective-permute-start | bytes 393224 | tf_op jit(solution)/shard_map/ppermute | solution.py:34
  318.5 6.5 %collective-permute-start.3 = (bf16[6,1,32,256]{3,2,1,0:T(8,128)(2,1)S(1)}, bf16[6,1,32,256]{3,2,1,0:T(8,128)(2,1)S(1)}, u32[]{:S(2)}, u32[]{:S(2)}) collective-permute-start(bf16[6,1,32,256]{3,2,1,0:T(8,128)(2,1)S(1)} %get-tuple-element.104), channel_id=1, source_target_pairs={{1,0},{2,1},{3,2},{5,4},{6,5},{7,6},{9,8},{10,9},{11,10},{13,12},{... | collective-permute-start | bytes 294920 | tf_op jit(solution)/shard_map/ppermute | solution.py:58
  319.8 6.8 %collective-permute-start.2 = (bf16[6,1,32,256]{3,2,1,0:T(8,128)(2,1)S(1)}, bf16[6,1,32,256]{3,2,1,0:T(8,128)(2,1)S(1)}, u32[]{:S(2)}, u32[]{:S(2)}) collective-permute-start(bf16[6,1,32,256]{3,2,1,0:T(8,128)(2,1)S(1)} %get-tuple-element.103), channel_id=1, source_target_pairs={{0,1},{1,2},{2,3},{4,5},{5,6},{6,7},{8,9},{9,10},{10,11},{12,13},{... | collective-permute-start | bytes 294920 | tf_op jit(solution)/shard_map/ppermute | solution.py:56
  330.8 106.5 %all-to-all-start.6 = ((f32[8,288,256]{2,1,0:T(8,128)}), f32[8,288,256]{2,1,0:T(8,128)S(1)}, u32[]{:S(2)}, u32[]{:S(2)}) async-start(f32[8,288,256]{2,1,0:T(8,128)} %bitcast.329), calls=%async_computation.6 | async-start | bytes 4718592 | tf_op jit(solution)/shard_map/all_to_all | solution.py:86
  345.0 97.2 %copy-start.5 = (f32[4,4,32,256]{3,2,1,0:T(8,128)S(1)}, f32[4,4,32,256]{3,2,1,0:T(8,128)}, u32[]{:S(2)}) copy-start(f32[4,4,32,256]{3,2,1,0:T(8,128)} %copy-done.4) | copy-start | bytes 1572868
  438.2 10.8 %all-to-all-start.7 = ((f32[4,72,256]{2,1,0:T(8,128)}), f32[4,72,256]{2,1,0:T(8,128)S(1)}, u32[]{:S(2)}, u32[]{:S(2)}) async-start(f32[4,72,256]{2,1,0:T(8,128)} %bitcast.332), calls=%async_computation.7 | async-start | bytes 589824 | tf_op jit(solution)/shard_map/all_to_all | solution.py:86
  (54 other events, 220.7 us)
Sparse Core Ops, SparseCore 0:
  61.5 69.8 all-gather.6
  133.5 96.3 all-gather.4
where the time goes:
time: 458 us; the launch traced here: 457 us
  waiting for transfers between devices  228 us (50%)
  starting transfers between devices  60.9 us (13%)
  blocking collectives  54.2 us (12%)
  local copies, waits for them, and re-layouts  41.6 us (9%)
  matrix products  40.5 us (9%)
  between operations  15.6 us (3%)
  other arithmetic  15.3 us (3%)
    all_to_all x2, waiting for transfers between devices, sum_at_owner(): lax.all_to_all(tiles, axis, split_axis=0, concat_axis=0, tiled=True)  97.7 us
    all_gather x1, waiting for transfers between devices, local(): latent_weight = lax.all_gather(conv_latent, 'tm', axis=0, tiled=True)  68.7 us
    all_gather x1, blocking collectives, gather_in_order(): tiles = lax.all_gather(tiles, axes[k])  54.2 us
    all_to_all x5, waiting for transfers between devices, copy_for_each(): lax.all_to_all(jnp.broadcast_to(array[None], (devices, *array.shape)), ax...  52.8 us
    all_to_all x5, starting transfers between devices, copy_for_each(): lax.all_to_all(jnp.broadcast_to(array[None], (devices, *array.shape)), ax...  29.7 us
    dot_general x54, matrix products, causal_taps(): jnp.dot(window.reshape(-1, channels_in), kernel, preferred_element_type=j...  20.3 us
    dot_general x27, matrix products, transposed_taps(): lax.dot_general(window.reshape(-1, channels_out), kernel, (((1,), (1,)),...  14 us
    all_to_all x2, starting transfers between devices, sum_at_owner(): lax.all_to_all(tiles, axis, split_axis=0, concat_axis=0, tiled=True)  9.22 us
  transfers between devices with their start and end apart: 17, of which 13 were waited for; matrix products, arithmetic and copies ran while one was open for 12% of the time, Pallas kernels for 0%

commit v1 on v0

--- a/solution.py
+++ b/solution.py
@@ -183,7 +183,8 @@
     extended = jnp.concatenate([earlier, active], 0)
     all_channels = gather_directly(extended, "height", 3)
     padded = jnp.pad(all_channels, ((0, 0), (1, 1), (1, 1), (0, 0)))
-    latent_weight = lax.all_gather(conv_latent, "tm", axis=0, tiled=True)
+    sent = jnp.stack([conv_latent] * lax.axis_size("tm"))
+    latent_weight = jnp.concatenate(lax.all_to_all(sent, "tm", 0, 0), axis=0)
     frames_latent, rows_latent, cols_latent = (latent.shape[0], latent.shape[1], latent.shape[2])
     mixed = causal_taps(padded, latent_weight, frames_latent, rows_latent, cols_latent)
     refined = (latent_f32 + mixed).astype(jnp.bfloat16)

time: 458 us -> 580 us (1.27)
  blocking collectives: 54.2 us -> 235 us
  waiting for transfers between devices: 228 us -> 154 us
  matrix products: 40.5 us -> 57.8 us
    all_gather x1, blocking collectives: 54.2 us -> 187 us  [gather_in_order(): tiles = lax.all_gather(tiles, axes[k])]
    all_gather x1 -> x0, waiting for transfers between devices: 68.7 us -> none  [local(): latent_weight = lax.all_gather(conv_latent, 'tm', axis=0, tiled=True)]
    all_to_all x0 -> x2, blocking collectives: none -> 48.1 us  [copy_for_each(): lax.all_to_all(jnp.broadcast_to(array[None], (devices, *array.shape)), ax...]
    all_to_all x5 -> x3, waiting for transfers between devices: 52.8 us -> 24 us  [copy_for_each(): lax.all_to_all(jnp.broadcast_to(array[None], (devices, *array.shape)), ax...]
    dot_general x54, matrix products: 20.3 us -> 37.6 us  [causal_taps(): jnp.dot(window.reshape(-1, channels_in), kernel, preferred_element_type=j...]
    all_gather x1, waiting for transfers between devices: 0.01 us -> 11.6 us  [gather_in_order(): tiles = lax.all_gather(tiles, axes[k])]
    all_to_all x5 -> x3, starting transfers between devices: 29.7 us -> 22.2 us  [copy_for_each(): lax.all_to_all(jnp.broadcast_to(array[None], (devices, *array.shape)), ax...]
    ppermute x3, waiting for transfers between devices: 3.41 us -> 9.92 us  [shifted(): return lax.ppermute(block, axis, route)]
  transfers between devices with their start and end apart: 17 -> 15, of which waited for: 13 -> 14; matrix products, arithmetic and copies ran while one was open for 12% -> 8% of each run, Pallas kernels for 0% -> 0%
where the time goes in v1:
time: 580 us; the launch traced here: 578 us
  blocking collectives  235 us (41%)
  waiting for transfers between devices  154 us (27%)
  starting transfers between devices  58 us (10%)
  matrix products  57.8 us (10%)
  local copies, waits for them, and re-layouts  41.9 us (7%)
  between operations  15.7 us (3%)
  other arithmetic  15.3 us (3%)
    all_gather x1, blocking collectives, gather_in_order(): tiles = lax.all_gather(tiles, axes[k])  187 us
    all_to_all x2, waiting for transfers between devices, sum_at_owner(): lax.all_to_all(tiles, axis, split_axis=0, concat_axis=0, tiled=True)  98.9 us
    all_to_all x2, blocking collectives, copy_for_each(): lax.all_to_all(jnp.broadcast_to(array[None], (devices, *array.shape)), ax...  48.1 us
    dot_general x54, matrix products, causal_taps(): jnp.dot(window.reshape(-1, channels_in), kernel, preferred_element_type=j...  37.6 us
    all_to_all x3, waiting for transfers between devices, copy_for_each(): lax.all_to_all(jnp.broadcast_to(array[None], (devices, *array.shape)), ax...  24 us
    all_to_all x3, starting transfers between devices, copy_for_each(): lax.all_to_all(jnp.broadcast_to(array[None], (devices, *array.shape)), ax...  22.2 us
    dot_general x27, matrix products, transposed_taps(): lax.dot_general(window.reshape(-1, channels_out), kernel, (((1,), (1,)),...  14.1 us
  transfers between devices with their start and end apart: 15, of which 14 were waited for; matrix products, arithmetic and copies ran while one was open for 8% of the time, Pallas kernels for 0%

profile of v1, /device:TPU:2, one launch (start us, length us, event | category | flops | bytes accessed | tf_op | source)
XLA Modules:
  0.0 577.9 jit_solution(16864679262984026640)
XLA Ops:
  8.5 22.7 %all_to_all.58 = f32[8,1,16]{2,1,0:T(1,128)S(1)} all-to-all(f32[8,1,16]{2,1,0:T(1,128)S(1)} %broadcast_in_dim.10), channel_id=1, replica_groups=mesh['dp'=16,'tm'=8,'height'=4] {'tm'}, dimensions={0} | all-to-all | bytes 1024 | tf_op jit(solution)/shard_map/all_to_all | solution.py:13
  37.9 4.5 all-to-all-start.1
  43.7 6.8 %all-to-all-done.1 = bf16[4,4,8,16,128]{4,3,2,1,0:T(8,128)(2,1)S(1)} async-done(((bf16[4,4,8,16,128]{4,3,2,1,0:T(8,128)(2,1)}), bf16[4,4,8,16,128]{4,3,2,1,0:T(8,128)(2,1)S(1)}, u32[]{:S(2)}, u32[]{:S(2)}) %all-to-all-start.1) | async-done | bytes 524320 | tf_op jit(solution)/shard_map/all_to_all | solution.py:13
  51.5 25.4 %all_to_all.59 = bf16[4,128,2048]{1,2,0:T(8,128)(2,1)S(1)} all-to-all(bf16[4,128,2048]{1,2,0:T(8,128)(2,1)S(1)} %broadcast_in_dim.12), channel_id=1, replica_groups=mesh['dp'=16,'tm'=8,'height'=4] {'height'}, dimensions={0} | all-to-all | bytes 4194304 | tf_op jit(solution)/shard_map/all_to_all | solution.py:13
  79.1 4.7 all-to-all-start.2
  83.8 187.2 %all-gather = bf16[1728,256]{1,0:T(8,128)(2,1)} all-gather(bf16[216,256]{1,0:T(8,128)(2,1)S(1)} %copy-done.59), channel_id=2, replica_groups=mesh['dp'=16,'tm'=8,'height'=4] {'tm'}, dimensions={0}, use_global_device_ids=true | all-gather | bytes 995328 | tf_op jit(solution)/shard_map/all_gather | solution.py:68
  272.4 5.5 collective-permute-done.4
  279.2 4.7 collective-permute-start.5
  284.5 3.3 collective-permute-done.5
  301.0 4.0 copy.76
  305.0 11.6 %all-gather.4.cloned.1.call-done = bf16[32,216,256]{2,1,0:T(8,128)(2,1)} async-done(((bf16[8,216,256]{2,1,0:T(8,128)(2,1)}), bf16[32,216,256]{2,1,0:T(8,128)(2,1)}) %all-gather.4.cloned.1.call-update) | async-done | bytes 3538960 | tf_op jit(solution)/shard_map/all_gather | solution.py:68
  359.3 3.9 all-to-all-start.3
  365.4 3.5 all-to-all-done.3
  371.9 3.7 fusion.146
  379.8 11.2 %all-to-all-start.5 = ((f32[32,1,64]{2,1,0:T(1,128)}), f32[32,1,64]{2,1,0:T(1,128)S(1)}, u32[]{:S(2)}, u32[]{:S(2)}) async-start(f32[32,1,64]{2,1,0:T(1,128)} %broadcast_in_dim.13), calls=%async_computation.5 | async-start | bytes 32768 | tf_op jit(solution)/shard_map/all_to_all | solution.py:13
  397.5 5.8 %all-to-all-done.5 = f32[32,1,64]{2,1,0:T(1,128)S(1)} async-done(((f32[32,1,64]{2,1,0:T(1,128)}), f32[32,1,64]{2,1,0:T(1,128)S(1)}, u32[]{:S(2)}, u32[]{:S(2)}) %all-to-all-start.5) | async-done | bytes 8224 | tf_op jit(solution)/shard_map/all_to_all | solution.py:13
  407.2 2.8 fusion.145
  410.7 6.6 %all-to-all-start.6 = ((f32[32,1,512]{2,1,0:T(1,128)}), f32[32,1,512]{2,1,0:T(1,128)S(1)}, u32[]{:S(2)}, u32[]{:S(2)}) async-start(f32[32,1,512]{2,1,0:T(1,128)} %broadcast_in_dim.14), calls=%async_computation.6 | async-start | bytes 131072 | tf_op jit(solution)/shard_map/all_to_all | solution.py:13
  418.7 11.5 %all-to-all-done.6 = f32[32,1,512]{2,1,0:T(1,128)S(1)} async-done(((f32[32,1,512]{2,1,0:T(1,128)}), f32[32,1,512]{2,1,0:T(1,128)S(1)}, u32[]{:S(2)}, u32[]{:S(2)}) %all-to-all-start.6) | async-done | bytes 65568 | tf_op jit(solution)/shard_map/all_to_all | solution.py:13
  439.9 4.6 collective-permute-start.2
  451.0 5.2 all-to-all-start.7
  465.9 92.8 %all-to-all-done.7 = f32[8,288,256]{2,1,0:T(8,128)S(1)} async-done(((f32[8,288,256]{2,1,0:T(8,128)}), f32[8,288,256]{2,1,0:T(8,128)S(1)}, u32[]{:S(2)}, u32[]{:S(2)}) %all-to-all-start.7) | async-done | bytes 2359328 | tf_op jit(solution)/shard_map/all_to_all | solution.py:86
  559.5 4.0 all-to-all-start.8
  564.3 6.1 %all-to-all-done.8 = f32[4,72,256]{2,1,0:T(8,128)S(1)} async-done(((f32[4,72,256]{2,1,0:T(8,128)}), f32[4,72,256]{2,1,0:T(8,128)S(1)}, u32[]{:S(2)}, u32[]{:S(2)}) %all-to-all-start.8) | async-done | bytes 294944 | tf_op jit(solution)/shard_map/all_to_all | solution.py:86
  (309 shorter events, 120.3 us)
Async XLA Ops:
  32.6 4.4 collective-permute-start
  37.9 12.5 %all-to-all-start.1 = ((bf16[4,4,8,16,128]{4,3,2,1,0:T(8,128)(2,1)}), bf16[4,4,8,16,128]{4,3,2,1,0:T(8,128)(2,1)S(1)}, u32[]{:S(2)}, u32[]{:S(2)}) async-start(bf16[4,4,8,16,128]{4,3,2,1,0:T(8,128)(2,1)} %broadcast_in_dim.11), calls=%async_computation.1 | async-start | bytes 1048576 | tf_op jit(solution)/shard_map/all_to_all | solution.py:13
  43.6 33.2 %copy-start.56 = (bf16[1728,128]{1,0:T(8,128)(2,1)S(1)}, bf16[1728,128]{1,0:T(8,128)(2,1)}, u32[]{:S(2)}) copy-start(bf16[1728,128]{1,0:T(8,128)(2,1)} %param.12) | copy-start | bytes 1327108
  79.1 191.9 %copy-start.6 = (bf16[4,4,32,256]{3,2,1,0:T(8,128)(2,1)S(1)}, bf16[4,4,32,256]{3,2,1,0:T(8,128)(2,1)}, u32[]{:S(2)}) copy-start(bf16[4,4,32,256]{3,2,1,0:T(8,128)(2,1)} %param.17) | copy-start | bytes 786436
  79.1 247.6 %all-to-all-start.2 = ((bf16[8,1728,128]{2,1,0:T(8,128)(2,1)}), bf16[8,1728,128]{2,1,0:T(8,128)(2,1)}, u32[]{:S(2)}, u32[]{:S(2)}) async-start(bf16[8,1728,128]{2,1,0:T(8,128)(2,1)} %stack.2), calls=%async_computation.2 | async-start | bytes 7077888 | tf_op jit(solution)/shard_map/all_to_all | solution.py:187
  83.8 232.8 %all-gather.4.cloned.1.call-start = ((), (), s32[]{:S(2)}) async-start(), calls=%async_computation.9 | async-start | bytes 4423680 | tf_op jit(solution)/shard_map/all_gather | solution.py:68
  271.0 6.9 %collective-permute-start.4 = (bf16[2,4,32,256]{3,2,1,0:T(8,128)(2,1)S(1)}, bf16[2,4,32,256]{3,2,1,0:T(8,128)(2,1)S(1)}, u32[]{:S(2)}, u32[]{:S(2)}) collective-permute-start(bf16[2,4,32,256]{3,2,1,0:T(8,128)(2,1)S(1)} %slice.629), channel_id=1, source_target_pairs={{4,0},{8,4},{12,8},{16,12},{20,16},{24,20},{28,24},{5,1},{9,5},{13... | collective-permute-start | bytes 393224 | tf_op jit(solution)/shard_map/ppermute | solution.py:34
  277.9 6.5 %collective-permute-start.6 = (bf16[6,1,32,256]{3,2,1,0:T(8,128)(2,1)S(1)}, bf16[6,1,32,256]{3,2,1,0:T(8,128)(2,1)S(1)}, u32[]{:S(2)}, u32[]{:S(2)}) collective-permute-start(bf16[6,1,32,256]{3,2,1,0:T(8,128)(2,1)S(1)} %get-tuple-element.98), channel_id=1, source_target_pairs={{1,0},{2,1},{3,2},{5,4},{6,5},{7,6},{9,8},{10,9},{11,10},{13,12},{... | collective-permute-start | bytes 294920 | tf_op jit(solution)/shard_map/ppermute | solution.py:58
  279.2 8.6 %collective-permute-start.5 = (bf16[6,1,32,256]{3,2,1,0:T(8,128)(2,1)S(1)}, bf16[6,1,32,256]{3,2,1,0:T(8,128)(2,1)S(1)}, u32[]{:S(2)}, u32[]{:S(2)}) collective-permute-start(bf16[6,1,32,256]{3,2,1,0:T(8,128)(2,1)S(1)} %get-tuple-element.97), channel_id=1, source_target_pairs={{0,1},{1,2},{2,3},{4,5},{5,6},{6,7},{8,9},{9,10},{10,11},{12,13},{... | collective-permute-start | bytes 294920 | tf_op jit(solution)/shard_map/ppermute | solution.py:56
  319.0 88.2 %copy-start = (bf16[8,4,216,256]{3,2,1,0:T(8,128)(2,1)}, bf16[8,4,216,256]{3,2,1,0:T(8,128)(2,1)S(1)}, u32[]{:S(2)}) copy-start(bf16[8,4,216,256]{3,2,1,0:T(8,128)(2,1)S(1)} %copy.79) | copy-start | bytes 10616836
  359.3 9.6 %all-to-all-start.3 = ((bf16[2,8,16,128]{3,2,0,1:T(8,128)(2,1)}), bf16[2,8,16,128]{3,2,0,1:T(8,128)(2,1)}, u32[]{:S(2)}, u32[]{:S(2)}) async-start(bf16[2,8,16,128]{3,2,0,1:T(8,128)(2,1)} %fusion.45), calls=%async_computation.3 | async-start | bytes 131072 | tf_op jit(solution)/shard_map/all_to_all | solution.py:192
  379.8 23.5 %all-to-all-start.5 = ((f32[32,1,64]{2,1,0:T(1,128)}), f32[32,1,64]{2,1,0:T(1,128)S(1)}, u32[]{:S(2)}, u32[]{:S(2)}) async-start(f32[32,1,64]{2,1,0:T(1,128)} %broadcast_in_dim.13), calls=%async_computation.5 | async-start | bytes 32768 | tf_op jit(solution)/shard_map/all_to_all | solution.py:13
  407.2 24.3 %copy-start.61 = (f32[256]{0:T(256)S(1)}, f32[256]{0:T(256)}, u32[]{:S(2)}) copy-start(f32[256]{0:T(256)} %mul.160) | copy-start | bytes 3076
  407.2 24.3 %copy-start.62 = (f32[256]{0:T(256)S(1)}, f32[256]{0:T(256)}, u32[]{:S(2)}) copy-start(f32[256]{0:T(256)} %sub.74) | copy-start | bytes 3076
  407.2 24.3 %copy-start.63 = (f32[256]{0:T(256)S(1)}, f32[256]{0:T(256)}, u32[]{:S(2)}) copy-start(f32[256]{0:T(256)} %param.15) | copy-start | bytes 3076
  410.0 37.0 %copy-start.8 = (bf16[4,4,32,256]{3,2,1,0:T(8,128)(2,1)S(1)}, bf16[4,4,32,256]{3,2,1,0:T(8,128)(2,1)}, u32[]{:S(2)}) copy-start(bf16[4,4,32,256]{3,2,1,0:T(8,128)(2,1)} %param.17) | copy-start | bytes 786436
  410.7 19.4 %all-to-all-start.6 = ((f32[32,1,512]{2,1,0:T(1,128)}), f32[32,1,512]{2,1,0:T(1,128)S(1)}, u32[]{:S(2)}, u32[]{:S(2)}) async-start(f32[32,1,512]{2,1,0:T(1,128)} %broadcast_in_dim.14), calls=%async_computation.6 | async-start | bytes 131072 | tf_op jit(solution)/shard_map/all_to_all | solution.py:13
  418.6 26.5 %copy-start.4 = (f32[4,4,32,256]{3,2,1,0:T(8,128)}, f32[4,4,32,256]{3,2,1,0:T(8,128)S(1)}, u32[]{:S(2)}) copy-start(f32[4,4,32,256]{3,2,1,0:T(8,128)S(1)} %reshape.490) | copy-start | bytes 1572868
  433.8 4.8 collective-permute-start.1
  438.6 6.5 %collective-permute-start.3 = (bf16[6,1,32,256]{3,2,1,0:T(8,128)(2,1)S(1)}, bf16[6,1,32,256]{3,2,1,0:T(8,128)(2,1)S(1)}, u32[]{:S(2)}, u32[]{:S(2)}) collective-permute-start(bf16[6,1,32,256]{3,2,1,0:T(8,128)(2,1)S(1)} %get-tuple-element.104), channel_id=1, source_target_pairs={{1,0},{2,1},{3,2},{5,4},{6,5},{7,6},{9,8},{10,9},{11,10},{13,12},{... | collective-permute-start | bytes 294920 | tf_op jit(solution)/shard_map/ppermute | solution.py:58
  439.9 6.8 %collective-permute-start.2 = (bf16[6,1,32,256]{3,2,1,0:T(8,128)(2,1)S(1)}, bf16[6,1,32,256]{3,2,1,0:T(8,128)(2,1)S(1)}, u32[]{:S(2)}, u32[]{:S(2)}) collective-permute-start(bf16[6,1,32,256]{3,2,1,0:T(8,128)(2,1)S(1)} %get-tuple-element.103), channel_id=1, source_target_pairs={{0,1},{1,2},{2,3},{4,5},{5,6},{6,7},{8,9},{9,10},{10,11},{12,13},{... | collective-permute-start | bytes 294920 | tf_op jit(solution)/shard_map/ppermute | solution.py:56
  451.0 107.7 %all-to-all-start.7 = ((f32[8,288,256]{2,1,0:T(8,128)}), f32[8,288,256]{2,1,0:T(8,128)S(1)}, u32[]{:S(2)}, u32[]{:S(2)}) async-start(f32[8,288,256]{2,1,0:T(8,128)} %bitcast.330), calls=%async_computation.7 | async-start | bytes 4718592 | tf_op jit(solution)/shard_map/all_to_all | solution.py:86
  465.2 98.3 %copy-start.5 = (f32[4,4,32,256]{3,2,1,0:T(8,128)S(1)}, f32[4,4,32,256]{3,2,1,0:T(8,128)}, u32[]{:S(2)}) copy-start(f32[4,4,32,256]{3,2,1,0:T(8,128)} %copy-done.4) | copy-start | bytes 1572868
  559.5 10.8 %all-to-all-start.8 = ((f32[4,72,256]{2,1,0:T(8,128)}), f32[4,72,256]{2,1,0:T(8,128)S(1)}, u32[]{:S(2)}, u32[]{:S(2)}) async-start(f32[4,72,256]{2,1,0:T(8,128)} %bitcast.333), calls=%async_computation.8 | async-start | bytes 589824 | tf_op jit(solution)/shard_map/all_to_all | solution.py:86
  (55 other events, 351.1 us)
Sparse Core Ops, SparseCore 0:
  271.1 45.4 all-gather.3
